TPU v7x, 32 devices: a whole 2x2x4 slice. The times are simulated.
32 devices in a mesh: rep: 2 (over x), node: 4 (over z), lane: 4 (over y, core).
Axes of the slice: x: 2, y: 2, z: 4, core: 2. Of those that a mesh axis runs over, the one named last changes fastest.
Arguments:
- moe_rows: bfloat16 [64, 7168], P(('rep', 'node', 'lane')), parts along dimension 0, may hold values from -6 to 6
- expert_ids: int32 [64, 8], P(('rep', 'node', 'lane')), parts along dimension 0, may hold values from 0 to 15, all different within a row; in each aligned block of 2 rows (0 to 1, 2 to 3, ...) at most 2 rows name the same one
- route_scores: float32 [64, 8], P(('rep', 'node', 'lane')), parts along dimension 0, may hold values from 0.05 to 1
- gate_proj: bfloat16 [16, 7168, 2048], P('lane', None, 'node'), may hold values from -0.0625 to 0.0625
- up_proj: bfloat16 [16, 7168, 2048], P('lane', None, 'node'), may hold values from -0.0625 to 0.0625
- down_proj: bfloat16 [16, 2048, 7168], P('lane', 'node'), may hold values from -0.125 to 0.125
Outputs:
- moe_out: bfloat16 [64, 7168], P(('rep', 'node', 'lane')), parts along dimension 0
There are 2 independent parts, one for each index of `rep`. A program takes and returns all parts, laid end to end along the dimension named above; an argument that names none is the same for every part. Nothing has to cross between parts.
Inputs may be any that keep to these rules, and one draw needn't show every extreme that they name: `expert_ids`: each row names 8 different experts; the rows of one device name no expert more than 2 times.
All inputs are finite; a program needn't handle non-finite values.
Results may differ from a plain program's by a relative error of at most 0.012.
Values may be sent and summed in bfloat16 or wider, within the bound.
A program may use at most 128 MiB of HBM per device.

v0:
```python
import jax
import jax.numpy as jnp
from jax import lax
from jax.sharding import PartitionSpec as P

TOP = 8
CAP = 2


route_factor = 2.5


def expert_ffn(slots_in, gate_proj, up_proj, down_proj):
    gate_val = jnp.einsum("kecd,edh->kech", slots_in, gate_proj, preferred_element_type=jnp.float32)
    up_val = jnp.einsum("kecd,edh->kech", slots_in, up_proj, preferred_element_type=jnp.float32)
    hidden = (jax.nn.silu(gate_val) * up_val).astype(jnp.bfloat16)
    return jnp.einsum("kech,ehd->kecd", hidden, down_proj, preferred_element_type=jnp.float32)


def on_device(moe_rows, expert_ids, route_scores, gate_proj, up_proj, down_proj):
    node_count = lax.axis_size("node")
    lane_count = lax.axis_size("lane")
    row_count, model_width = moe_rows.shape
    local_experts = gate_proj.shape[0]
    experts = local_experts * lane_count
    slot_total = experts * CAP
    weights = route_factor * route_scores / jnp.sum(route_scores, axis=1, keepdims=True)
    onehot = (expert_ids[:, :, None] == jnp.arange(experts, dtype=jnp.int32)[None, None, :]).astype(
        jnp.int32
    )
    flat_hits = onehot.reshape((row_count * TOP, experts))
    earlier = jnp.cumsum(flat_hits, axis=0) - flat_hits
    slot_rank = jnp.sum(earlier * flat_hits, axis=1).reshape((row_count, TOP))
    position = expert_ids * CAP + slot_rank
    picked = (
        position[:, :, None] == jnp.arange(slot_total, dtype=jnp.int32)[None, None, :]
    ).astype(jnp.float32)
    dispatch_mat = jnp.max(picked, axis=1).T.astype(jnp.bfloat16)
    combine_mat = jnp.sum(weights[:, :, None] * picked, axis=1)
    send_flat = jnp.dot(dispatch_mat, moe_rows, preferred_element_type=jnp.float32).astype(
        jnp.bfloat16
    )
    send_block = send_flat.reshape((lane_count, local_experts, CAP, model_width))
    copies = jnp.broadcast_to(send_block[None], (node_count,) + send_block.shape)
    copies = copies.reshape((node_count * lane_count, local_experts, CAP, model_width))
    partial_value = expert_ffn(
        lax.all_to_all(copies, ("node", "lane"), split_axis=0, concat_axis=0, tiled=True),
        gate_proj,
        up_proj,
        down_proj,
    )
    returned = lax.all_to_all(
        partial_value.astype(jnp.bfloat16),
        ("node", "lane"),
        split_axis=0,
        concat_axis=0,
        tiled=True,
    )
    returned = returned.astype(jnp.float32).reshape((node_count, experts, CAP, model_width))
    expert_out = jnp.sum(returned, axis=0)
    moe_out = jnp.dot(
        combine_mat,
        expert_out.reshape((slot_total, model_width)),
        precision=lax.Precision.HIGHEST,
        preferred_element_type=jnp.float32,
    )
    return moe_out.astype(jnp.bfloat16)


def solution(mesh):
    in_specs = (
        P(("rep", "node", "lane"), None),
        P(("rep", "node", "lane"), None),
        P(("rep", "node", "lane"), None),
        P("lane", None, "node"),
        P("lane", None, "node"),
        P("lane", "node", None),
    )
    out_specs = P(("rep", "node", "lane"), None)
    return jax.shard_map(
        on_device, mesh=mesh, in_specs=in_specs, out_specs=out_specs, check_vma=False
    )
```

profile of v0, /device:TPU:0, one launch (start us, length us, event | category | flops | bytes accessed | tf_op | source)
XLA Modules:
  0.0 146.4 jit_solution(15134382568448264485)
XLA Ops:
  0.0 0.0 copy-start
  0.0 0.8 eq.29
  0.8 0.8 reduce_sum.37
  1.6 0.7 multiply_divide_fusion
  2.3 0.1 fusion.34
  2.4 0.2 select_reduce_fusion.1
  2.6 0.1 reshape.23
  2.7 0.7 multiply_add_fusion
  3.4 0.1 convert_reduce_fusion.1
  3.5 0.0 copy-done
  3.5 0.3 convolution_convert_fusion
  3.8 0.2 broadcast_in_dim.4
  4.0 1.4 broadcast_in_dim.5
  5.4 49.9 %all_to_all.10 = bf16[16,4,2,7168]{3,2,1,0:T(2,128)(2,1)S(1)} all-to-all(bf16[16,4,2,7168]{3,2,1,0:T(2,128)(2,1)S(1)} %bitcast.47), channel_id=1, replica_groups=mesh['rep'=2,'node'=4,'lane'=4] {'node','lane'}, dimensions={0} | all-to-all | bytes 3670016 | tf_op jit(solution)/shard_map/all_to_all | solution.py:47
  55.4 12.1 %fusion.14 = f32[16,4,2,512]{3,0,2,1:T(8,128)S(1)} fusion(bf16[4,7168,512]{2,1,0:T(8,128)(2,1)} %param.9, bf16[16,4,2,7168]{3,2,1,0:T(2,128)(2,1)S(1)} %all_to_all.10), kind=kOutput, calls=%fused_computation.13 | convolution fusion | flops 939524096 | bytes 31457280 | tf_op jit(solution)/shard_map/kecd,edh->kech/dot_general | solution.py:14
  67.5 12.2 %fusion.29 = bf16[16,4,2,512]{3,0,2,1:T(8,128)(2,1)S(1)} fusion(bf16[4,7168,512]{2,1,0:T(8,128)(2,1)} %param.10, bf16[16,4,2,7168]{3,2,1,0:T(2,128)(2,1)S(1)} %all_to_all.10, f32[16,4,2,512]{3,0,2,1:T(8,128)S(1)} %fusion.14), kind=kOutput, calls=%fused_computation.16 | convolution fusion | flops 939917312 | bytes 31588352 | tf_op jit(solution)/shard_map/kecd,edh->kech/dot_general | solution.py:15
  79.7 14.6 %fusion.9 = bf16[16,4,2,7168]{3,0,2,1:T(8,128)(2,1)S(1)} fusion(bf16[16,4,2,512]{3,0,2,1:T(8,128)(2,1)S(1)} %fusion.29, bf16[4,512,7168]{2,1,0:T(8,128)(2,1)} %param.11), kind=kOutput, calls=%fused_computation.7 | convolution fusion | flops 940441600 | bytes 31326208 | tf_op jit(solution)/shard_map/kech,ehd->kecd/dot_general | solution.py:17
  94.4 1.9 %copy.15 = bf16[16,4,2,7168]{3,2,1,0:T(2,128)(2,1)S(1)} copy(bf16[16,4,2,7168]{3,0,2,1:T(8,128)(2,1)S(1)} %fusion.9) | data formatting | bytes 3670016 | tf_op jit(solution)/shard_map/convert_element_type | solution.py:53
  96.3 46.6 %all_to_all.11 = bf16[16,4,2,7168]{3,2,1,0:T(2,128)(2,1)S(1)} all-to-all(bf16[16,4,2,7168]{3,2,1,0:T(2,128)(2,1)S(1)} %copy.15), channel_id=1, replica_groups=mesh['rep'=2,'node'=4,'lane'=4] {'node','lane'}, dimensions={0} | all-to-all | bytes 3670016 | tf_op jit(solution)/shard_map/all_to_all | solution.py:52
  142.8 0.0 copy-start.1
  142.8 1.7 %convert_reduce_fusion = f32[16,2,7168]{2,1,0:T(2,128)S(1)} fusion(bf16[4,16,2,7168]{3,2,1,0:T(2,128)(2,1)S(1)} %bitcast.48), kind=kLoop, calls=%fused_computation.10 | loop fusion | flops 1605632 | bytes 2752512 | tf_op jit(solution)/shard_map/reduce_sum | solution.py:60
  144.6 0.6 reshape.27
  145.2 1.2 convolution_convert_fusion.1
  146.4 0.0 copy-done.1
  (1 shorter events, 0.0 us)
Async XLA Ops:
  0.0 3.5 %copy-start = (bf16[2,7168]{1,0:T(2,128)(2,1)S(1)}, bf16[2,7168]{1,0:T(2,128)(2,1)}, u32[]{:S(2)}) copy-start(bf16[2,7168]{1,0:T(2,128)(2,1)} %param.6) | copy-start | bytes 86020
  142.8 3.6 %copy-start.1 = (bf16[2,7168]{1,0:T(2,128)(2,1)S(1)}, bf16[2,7168]{1,0:T(2,128)(2,1)}, u32[]{:S(2)}) copy-start(bf16[2,7168]{1,0:T(2,128)(2,1)} %param.6) | copy-start | bytes 86020
where the time goes:
time: 147 us; the launch traced here: 146 us
  blocking collectives  96.5 us (66%)
  matrix products  40.5 us (28%)
  local copies, waits for them, and re-layouts  4.97 us (3%)
  other arithmetic  4.36 us (3%)
    all_to_all x1, blocking collectives, on_device(): lax.all_to_all(copies, ('node', 'lane'), split_axis=0, concat_axis=0, til...  49.9 us
    all_to_all x1, blocking collectives, on_device(): lax.all_to_all(partial_value.astype(jnp.bfloat16), ('node', 'lane'), spli...  46.6 us
    dot_general x1, matrix products, expert_ffn(): jnp.einsum('kech,ehd->kecd', hidden, down_proj, preferred_element_type=jn...  14.6 us
    dot_general x1, matrix products, expert_ffn(): jnp.einsum('kecd,edh->kech', slots_in, up_proj, preferred_element_type=jn...  12.2 us
    dot_general x1, matrix products, expert_ffn(): jnp.einsum('kecd,edh->kech', slots_in, gate_proj, preferred_element_type=...  12.1 us

commit v1 on v0

v1 whole, which is shorter than its diff:
```python
import functools

import jax
import jax.numpy as jnp
from jax import lax
from jax.experimental import pallas as pl
from jax.experimental.pallas import tpu as pltpu
from jax.sharding import PartitionSpec as P

route_factor = 2.5
MESH = pl.DeviceIdType.MESH
LANES = 128
RING = 16
DOWN_RING = 3


def kernel(
    cfg, rows_ref, ids_ref, scores_ref, gate_hbm, up_hbm, down_hbm, out_ref,
    gate_buf, up_buf, down_buf, pack, mine, gathered, wide, x_buf, w_buf,
    gate_acc, up_acc, hidden, part_buf, send_buf, recv_buf, total,
    gate_sem, up_sem, down_sem, gs_sem, gr_sem, rs_sem, rr_sem,
):
    nodes, lanes, k_step, c_step, stride = cfg
    n = nodes * lanes
    t_dev, width = rows_ref.shape
    experts_here, _, units = gate_hbm.shape
    pieces = width // LANES
    k_steps, c_steps = width // k_step, width // c_step
    steps = experts_here * k_steps
    ring, down_ring = gate_buf.shape[0], down_buf.shape[0]
    per_chunk = c_step // LANES
    block = t_dev * stride
    back = t_dev * per_chunk
    tokens = n * t_dev
    node, lane = lax.axis_index("node"), lax.axis_index("lane")
    me = node * lanes + lane

    def gate_up(step):
        slot = lax.rem(step, ring)
        e, k = step // k_steps, lax.rem(step, k_steps)
        at = pl.ds(pl.multiple_of(k * k_step, k_step), k_step)
        return (
            pltpu.make_async_copy(gate_hbm.at[e, at, :], gate_buf.at[slot], gate_sem.at[slot]),
            pltpu.make_async_copy(up_hbm.at[e, at, :], up_buf.at[slot], up_sem.at[slot]),
        )

    def down(q):
        slot = lax.rem(q, down_ring)
        at = pl.ds(pl.multiple_of(q * c_step, c_step), c_step)
        return pltpu.make_async_copy(down_hbm.at[:, :, at], down_buf.at[slot], down_sem.at[slot])

    def peer(s):
        p = lax.rem(me + s, n)
        return p, {"node": p // lanes, "lane": lax.rem(p, lanes)}

    def start_step(step, _=None):
        for copy in gate_up(step):
            copy.start()
        return 0

    ahead = min(ring, steps)
    lax.fori_loop(0, ahead, start_step, 0)

    barrier = pltpu.get_barrier_semaphore()

    def greet(s, _):
        pl.semaphore_signal(barrier, inc=1, device_id=peer(s)[1], device_id_type=MESH)
        return 0

    lax.fori_loop(1, n, greet, 0)

    ids, scores = ids_ref[...], scores_ref[...]
    weights = route_factor * scores / jnp.sum(scores, axis=1, keepdims=True)
    column = lax.broadcasted_iota(jnp.int32, (t_dev, LANES), 1)
    dense = jnp.zeros((t_dev, LANES), jnp.float32)
    for k in range(ids.shape[1]):
        dense = dense + jnp.where(column == ids[:, k:k + 1], weights[:, k:k + 1], 0.0)
    high = dense.astype(jnp.bfloat16).astype(jnp.float32)
    low = dense - high
    pack[...] = jnp.zeros_like(pack)
    own = rows_ref[...].astype(jnp.float32)
    for i in range(t_dev):
        for c in range(pieces):
            pack[i * stride + c:i * stride + c + 1, :] = own[i:i + 1, c * LANES:(c + 1) * LANES]
        pack[i * stride + pieces:i * stride + pieces + 1, :] = high[i:i + 1, :]
        pack[i * stride + pieces + 1:i * stride + pieces + 2, :] = low[i:i + 1, :]
    packed = pack[...].astype(jnp.bfloat16)
    mine[...] = packed
    gathered[me] = packed

    pl.semaphore_wait(barrier, n - 1)

    def spread(s):
        p, device = peer(s)
        return pltpu.make_async_remote_copy(
            src_ref=mine, dst_ref=gathered.at[me], send_sem=gs_sem.at[s], recv_sem=gr_sem.at[s],
            device_id=device, device_id_type=MESH,
        )

    def spread_start(s, _):
        spread(s).start()
        return 0

    lax.fori_loop(1, n, spread_start, 0)

    def arrive(s, _):
        spread(s).wait_recv()
        return 0

    lax.fori_loop(1, n, arrive, 0)

    def widen(p, _):
        wide[pl.ds(pl.multiple_of(p * block, block), block), :] = gathered[p].astype(jnp.float32)
        return 0

    lax.fori_loop(0, n, widen, 0)
    for c in range(pieces):
        at = c * LANES
        x_buf[at // k_step, :, at % k_step:at % k_step + LANES] = wide[
            pl.ds(c, tokens, stride=stride), :
        ].astype(jnp.bfloat16)
    w_buf[...] = wide[pl.ds(pieces, tokens, stride=stride), :] + wide[pl.ds(pieces + 1, tokens, stride=stride), :]

    def one_expert(e, _):
        gate_acc[...] = jnp.zeros_like(gate_acc)
        up_acc[...] = jnp.zeros_like(up_acc)

        def one_step(k, _):
            step = e * k_steps + k
            slot = lax.rem(step, ring)
            for copy in gate_up(step):
                copy.wait()
            x = x_buf[k]
            gate_acc[...] += jnp.dot(x, gate_buf[slot], preferred_element_type=jnp.float32)
            up_acc[...] += jnp.dot(x, up_buf[slot], preferred_element_type=jnp.float32)

            @pl.when(step + ring < steps)
            def _():
                start_step(step + ring)

            for q in range(min(down_ring, c_steps)):
                @pl.when(step == max(steps - ring, 0) + q)
                def _():
                    down(q).start()

            return 0

        lax.fori_loop(0, k_steps, one_step, 0)
        pick = lax.broadcasted_iota(jnp.int32, w_buf.shape, 1) == lane * experts_here + e
        weight = jnp.sum(jnp.where(pick, w_buf[...], 0.0), axis=1, keepdims=True)
        g = gate_acc[...]
        hidden[e] = (weight * (g / (1.0 + jnp.exp(-g)) * up_acc[...])).astype(jnp.bfloat16)
        return 0

    lax.fori_loop(0, experts_here, one_expert, 0)

    def give(q, s):
        p, device = peer(s)
        return pltpu.make_async_remote_copy(
            src_ref=send_buf.at[q, p], dst_ref=recv_buf.at[q, me],
            send_sem=rs_sem.at[q, s], recv_sem=rr_sem.at[q, s],
            device_id=device, device_id_type=MESH,
        )

    def one_chunk(q, _):
        slot = lax.rem(q, down_ring)
        down(q).wait()
        part = jnp.dot(hidden[0], down_buf[slot, 0], preferred_element_type=jnp.float32)
        for e in range(1, experts_here):
            part = part + jnp.dot(hidden[e], down_buf[slot, e], preferred_element_type=jnp.float32)
        for c in range(per_chunk):
            part_buf[pl.ds(c, tokens, stride=per_chunk), :] = part[:, c * LANES:(c + 1) * LANES]
        send_buf[q] = part_buf[...].astype(jnp.bfloat16).reshape((n, back, LANES))

        @pl.when(q + down_ring < c_steps)
        def _():
            down(q + down_ring).start()

        def give_start(s, _):
            give(q, s).start()
            return 0

        lax.fori_loop(1, n, give_start, 0)
        return 0

    lax.fori_loop(0, c_steps, one_chunk, 0)

    def sum_chunk(q, _):
        def taken(s, _):
            give(q, s).wait_recv()
            return 0

        lax.fori_loop(1, n, taken, 0)
        recv_buf[q, me] = send_buf[q, me]
        total[pl.ds(pl.multiple_of(q * back, back), back), :] = jnp.sum(
            recv_buf[q].astype(jnp.float32), axis=0
        )
        return 0

    lax.fori_loop(0, c_steps, sum_chunk, 0)
    for q in range(c_steps):
        for c in range(per_chunk):
            at = q * c_step + c * LANES
            out_ref[:, at:at + LANES] = total[pl.ds(q * back + c, t_dev, stride=per_chunk), :].astype(out_ref.dtype)

    def left(s, _):
        spread(s).wait_send()

        def each(q, _):
            give(q, s).wait_send()
            return 0

        lax.fori_loop(0, c_steps, each, 0)
        return 0

    lax.fori_loop(1, n, left, 0)


def on_device(moe_rows, expert_ids, route_scores, gate_proj, up_proj, down_proj):
    nodes, lanes = lax.axis_size("node"), lax.axis_size("lane")
    n = nodes * lanes
    t_dev, width = moe_rows.shape
    experts_here, _, units = gate_proj.shape
    k_step = c_step = 1024
    stride = -(-(width // LANES + 2) // 16) * 16
    tokens = n * t_dev
    per_chunk = c_step // LANES
    ring = min(RING, experts_here * (width // k_step))
    down_ring = min(DOWN_RING, width // c_step)
    bf16, f32 = jnp.bfloat16, jnp.float32
    vmem, hbm = pl.BlockSpec(memory_space=pltpu.VMEM), pl.BlockSpec(memory_space=pl.ANY)
    return pl.pallas_call(
        functools.partial(kernel, (nodes, lanes, k_step, c_step, stride)),
        out_shape=jax.ShapeDtypeStruct((t_dev, width), bf16),
        in_specs=[vmem, vmem, vmem, hbm, hbm, hbm],
        out_specs=vmem,
        scratch_shapes=[
            pltpu.VMEM((ring, k_step, units), bf16),
            pltpu.VMEM((ring, k_step, units), bf16),
            pltpu.VMEM((down_ring, experts_here, units, c_step), bf16),
            pltpu.VMEM((t_dev * stride, LANES), f32),
            pltpu.VMEM((t_dev * stride, LANES), bf16),
            pltpu.VMEM((n, t_dev * stride, LANES), bf16),
            pltpu.VMEM((tokens * stride, LANES), f32),
            pltpu.VMEM((width // k_step, tokens, k_step), bf16),
            pltpu.VMEM((tokens, LANES), f32),
            pltpu.VMEM((tokens, units), f32),
            pltpu.VMEM((tokens, units), f32),
            pltpu.VMEM((experts_here, tokens, units), bf16),
            pltpu.VMEM((tokens * per_chunk, LANES), f32),
            pltpu.VMEM((width // c_step, n, t_dev * per_chunk, LANES), bf16),
            pltpu.VMEM((width // c_step, n, t_dev * per_chunk, LANES), bf16),
            pltpu.VMEM((t_dev * width // LANES, LANES), f32),
            pltpu.SemaphoreType.DMA((ring,)),
            pltpu.SemaphoreType.DMA((ring,)),
            pltpu.SemaphoreType.DMA((down_ring,)),
            pltpu.SemaphoreType.DMA((n,)),
            pltpu.SemaphoreType.DMA((n,)),
            pltpu.SemaphoreType.DMA((width // c_step, n)),
            pltpu.SemaphoreType.DMA((width // c_step, n)),
        ],
        compiler_params=pltpu.CompilerParams(
            collective_id=0, has_side_effects=True, vmem_limit_bytes=60 * 2**20
        ),
        cost_estimate=pl.CostEstimate(
            flops=6 * tokens * experts_here * width * units,
            bytes_accessed=6 * experts_here * width * units,
            transcendentals=tokens * experts_here * units,
        ),
    )(moe_rows, expert_ids, route_scores, gate_proj, up_proj, down_proj)


def solution(mesh):
    in_specs = (
        P(("rep", "node", "lane"), None),
        P(("rep", "node", "lane"), None),
        P(("rep", "node", "lane"), None),
        P("lane", None, "node"),
        P("lane", None, "node"),
        P("lane", "node", None),
    )
    out_specs = P(("rep", "node", "lane"), None)
    return jax.shard_map(
        on_device, mesh=mesh, in_specs=in_specs, out_specs=out_specs, check_vma=False
    )
```

time: 147 us -> 51.9 us (0.35)
  blocking collectives: 96.5 us -> 0 us
  Pallas kernels: 0 us -> 50.3 us
  matrix products: 40.5 us -> 0 us
  other arithmetic: 4.36 us -> 0 us
  local copies, waits for them, and re-layouts: 4.97 us -> 1.38 us
    all_to_all x2 -> x0, blocking collectives: 96.5 us -> none  [the longest x1 49.9 us: on_device(): lax.all_to_all(copies, ('node', 'lane'), split_axis=0, concat_axis=0, til...]
    pallas_call x0 -> x1, Pallas kernels: none -> 50.3 us  [on_device(): pl.pallas_call(functools.partial(kernel, (nodes, lanes, k_step, c_step, s...]
    dot_general x5 -> x0, matrix products: 40.5 us -> none  [the longest x1 14.6 us: expert_ffn(): jnp.einsum('kech,ehd->kecd', hidden, down_proj, preferred_element_type=jn...]
    reduce_sum x3 -> x0, other arithmetic: 2.72 us -> none  [the longest x1 1.74 us: on_device(): expert_out = jnp.sum(returned, axis=0)]
    convert_element_type x1 -> x0, local copies, waits for them, and re-layouts: 1.9 us -> none  [on_device(): partial_value.astype(jnp.bfloat16)]
    broadcast_in_dim x2 -> x0, local copies, waits for them, and re-layouts: 1.58 us -> none  [on_device(): jnp.broadcast_to(send_block[None], (node_count,) + send_block.shape)]
where the time goes in v1:
time: 51.9 us; the launch traced here: 51.6 us
  Pallas kernels  50.3 us (97%)
  local copies, waits for them, and re-layouts  1.38 us (3%)
    pallas_call x1, Pallas kernels, on_device(): pl.pallas_call(functools.partial(kernel, (nodes, lanes, k_step, c_step, s...  50.3 us
    unnamed x1, local copies, waits for them, and re-layouts  1.38 us

profile of v1, /device:TPU:0, one launch (start us, length us, event | category | flops | bytes accessed | tf_op | source)
XLA Modules:
  0.0 51.6 jit_solution(5928741629769705057)
XLA Ops:
  0.0 50.3 %shard_map.64 = bf16[2,7168]{1,0:T(2,128)(2,1)} custom-call(bf16[2,7168]{1,0:T(2,128)(2,1)} %rows_ref.1, s32[2,8]{1,0:T(2,128)} %ids_ref.1, f32[2,8]{1,0:T(2,128)} %scores_ref.1, bf16[4,7168,512]{2,1,0:T(8,128)(2,1)} %gate_hbm.1, bf16[4,7168,512]{2,1,0:T(8,128)(2,1)} %up_hbm.1, bf16[4,512,7168]{2,1,0:T(8,128)(2,1)} %down_hbm.1), custom_call_target="tpu_custom_call" | custom-call | flops 2818572288 | bytes 88080384 | tf_op jit(solution)/shard_map/pallas_call | solution.py:232
  50.3 1.4 %copy.8 = bf16[2,7168]{1,0:T(2,128)(2,1)} copy(bf16[2,7168]{1,0:T(2,128)(2,1)} %shard_map.64) | data formatting | bytes 57344

commit v2 on v1

--- a/solution.py
+++ b/solution.py
@@ -10,15 +10,17 @@
 route_factor = 2.5
 MESH = pl.DeviceIdType.MESH
 LANES = 128
-RING = 16
+RING = 20
 DOWN_RING = 3
+LAG = 3
+FIRST = 5
 
 
 def kernel(
     cfg, rows_ref, ids_ref, scores_ref, gate_hbm, up_hbm, down_hbm, out_ref,
-    gate_buf, up_buf, down_buf, pack, mine, gathered, wide, x_buf, w_buf,
-    gate_acc, up_acc, hidden, part_buf, send_buf, recv_buf, total,
-    gate_sem, up_sem, down_sem, gs_sem, gr_sem, rs_sem, rr_sem,
+    gate_buf, up_buf, down_buf, pack, gathered, wide, x_buf, w_buf,
+    gate_acc, up_acc, hidden, part_buf, lane_out, lane_in, node_out, node_in, total,
+    gate_sem, up_sem, down_sem, zs_sem, zr_sem, fs_sem, fr_sem, ls_sem, lr_sem, ns_sem, nr_sem,
 ):
     nodes, lanes, k_step, c_step, stride = cfg
     n = nodes * lanes
@@ -33,7 +35,6 @@
     back = t_dev * per_chunk
     tokens = n * t_dev
     node, lane = lax.axis_index("node"), lax.axis_index("lane")
-    me = node * lanes + lane
 
     def gate_up(step):
         slot = lax.rem(step, ring)
@@ -49,25 +50,27 @@
         at = pl.ds(pl.multiple_of(q * c_step, c_step), c_step)
         return pltpu.make_async_copy(down_hbm.at[:, :, at], down_buf.at[slot], down_sem.at[slot])
 
-    def peer(s):
-        p = lax.rem(me + s, n)
-        return p, {"node": p // lanes, "lane": lax.rem(p, lanes)}
+    def node_at(s):
+        return lax.rem(node + s, nodes)
+
+    def lane_at(s):
+        return lax.rem(lane + s, lanes)
 
     def start_step(step, _=None):
         for copy in gate_up(step):
             copy.start()
         return 0
 
+    barrier = pltpu.get_barrier_semaphore()
+
+    for s in range(1, nodes):
+        pl.semaphore_signal(barrier, inc=1, device_id={"node": node_at(s)}, device_id_type=MESH)
+    for s in range(1, lanes):
+        pl.semaphore_signal(barrier, inc=1, device_id={"lane": lane_at(s)}, device_id_type=MESH)
+
     ahead = min(ring, steps)
-    lax.fori_loop(0, ahead, start_step, 0)
-
-    barrier = pltpu.get_barrier_semaphore()
-
-    def greet(s, _):
-        pl.semaphore_signal(barrier, inc=1, device_id=peer(s)[1], device_id_type=MESH)
-        return 0
-
-    lax.fori_loop(1, n, greet, 0)
+    first = min(FIRST, ahead)
+    lax.fori_loop(0, first, start_step, 0)
 
     ids, scores = ids_ref[...], scores_ref[...]
     weights = route_factor * scores / jnp.sum(scores, axis=1, keepdims=True)
@@ -84,30 +87,39 @@
             pack[i * stride + c:i * stride + c + 1, :] = own[i:i + 1, c * LANES:(c + 1) * LANES]
         pack[i * stride + pieces:i * stride + pieces + 1, :] = high[i:i + 1, :]
         pack[i * stride + pieces + 1:i * stride + pieces + 2, :] = low[i:i + 1, :]
-    packed = pack[...].astype(jnp.bfloat16)
-    mine[...] = packed
-    gathered[me] = packed
-
-    pl.semaphore_wait(barrier, n - 1)
-
-    def spread(s):
-        p, device = peer(s)
+    gathered[lane * nodes + node] = pack[...].astype(jnp.bfloat16)
+
+    pl.semaphore_wait(barrier, nodes + lanes - 2)
+
+    def across(s):
         return pltpu.make_async_remote_copy(
-            src_ref=mine, dst_ref=gathered.at[me], send_sem=gs_sem.at[s], recv_sem=gr_sem.at[s],
-            device_id=device, device_id_type=MESH,
-        )
-
-    def spread_start(s, _):
-        spread(s).start()
-        return 0
-
-    lax.fori_loop(1, n, spread_start, 0)
-
-    def arrive(s, _):
-        spread(s).wait_recv()
-        return 0
-
-    lax.fori_loop(1, n, arrive, 0)
+            src_ref=gathered.at[lane * nodes + node], dst_ref=gathered.at[lane * nodes + node],
+            send_sem=zs_sem.at[s], recv_sem=zr_sem.at[s],
+            device_id={"node": node_at(s)}, device_id_type=MESH,
+        )
+
+    def forward(s, t):
+        at = lane * nodes + node_at(nodes - s)
+        return pltpu.make_async_remote_copy(
+            src_ref=gathered.at[at], dst_ref=gathered.at[at],
+            send_sem=fs_sem.at[s, t], recv_sem=fr_sem.at[s, t],
+            device_id={"lane": lane_at(t)}, device_id_type=MESH,
+        )
+
+    for s in range(1, nodes):
+        across(s).start()
+    for t in range(1, lanes):
+        forward(0, t).start()
+    lax.fori_loop(first, ahead, start_step, 0)
+    for q in range(down_ring):
+        down(q).start()
+    for s in range(1, nodes):
+        across(s).wait_recv()
+        for t in range(1, lanes):
+            forward(s, t).start()
+    for s in range(nodes):
+        for t in range(1, lanes):
+            forward(s, t).wait_recv()
 
     def widen(p, _):
         wide[pl.ds(pl.multiple_of(p * block, block), block), :] = gathered[p].astype(jnp.float32)
@@ -138,11 +150,6 @@
             def _():
                 start_step(step + ring)
 
-            for q in range(min(down_ring, c_steps)):
-                @pl.when(step == max(steps - ring, 0) + q)
-                def _():
-                    down(q).start()
-
             return 0
 
         lax.fori_loop(0, k_steps, one_step, 0)
@@ -154,13 +161,28 @@
 
     lax.fori_loop(0, experts_here, one_expert, 0)
 
-    def give(q, s):
-        p, device = peer(s)
+    def to_lane(q, s):
         return pltpu.make_async_remote_copy(
-            src_ref=send_buf.at[q, p], dst_ref=recv_buf.at[q, me],
-            send_sem=rs_sem.at[q, s], recv_sem=rr_sem.at[q, s],
-            device_id=device, device_id_type=MESH,
-        )
+            src_ref=lane_out.at[q, lane_at(s)], dst_ref=lane_in.at[q, lane],
+            send_sem=ls_sem.at[q, s], recv_sem=lr_sem.at[q, s],
+            device_id={"lane": lane_at(s)}, device_id_type=MESH,
+        )
+
+    def to_node(q, s):
+        return pltpu.make_async_remote_copy(
+            src_ref=node_out.at[q, node_at(s)], dst_ref=node_in.at[q, node],
+            send_sem=ns_sem.at[q, s], recv_sem=nr_sem.at[q, s],
+            device_id={"node": node_at(s)}, device_id_type=MESH,
+        )
+
+    def lane_sum(q):
+        for s in range(1, lanes):
+            to_lane(q, s).wait_recv()
+        lane_in[q, lane] = lane_out[q, lane]
+        summed = jnp.sum(lane_in[q].astype(jnp.float32), axis=0)
+        node_out[q] = summed.astype(jnp.bfloat16).reshape((nodes, back, LANES))
+        for s in range(1, nodes):
+            to_node(q, s).start()
 
     def one_chunk(q, _):
         slot = lax.rem(q, down_ring)
@@ -170,30 +192,34 @@
             part = part + jnp.dot(hidden[e], down_buf[slot, e], preferred_element_type=jnp.float32)
         for c in range(per_chunk):
             part_buf[pl.ds(c, tokens, stride=per_chunk), :] = part[:, c * LANES:(c + 1) * LANES]
-        send_buf[q] = part_buf[...].astype(jnp.bfloat16).reshape((n, back, LANES))
+        lane_out[q] = part_buf[...].astype(jnp.bfloat16).reshape((lanes, nodes * back, LANES))
+        for s in range(1, lanes):
+            to_lane(q, s).start()
 
         @pl.when(q + down_ring < c_steps)
         def _():
             down(q + down_ring).start()
 
-        def give_start(s, _):
-            give(q, s).start()
-            return 0
-
-        lax.fori_loop(1, n, give_start, 0)
+        @pl.when(q >= LAG)
+        def _():
+            lane_sum(q - LAG)
+
         return 0
 
     lax.fori_loop(0, c_steps, one_chunk, 0)
 
+    def late(q, _):
+        lane_sum(q)
+        return 0
+
+    lax.fori_loop(max(c_steps - LAG, 0), c_steps, late, 0)
+
     def sum_chunk(q, _):
-        def taken(s, _):
-            give(q, s).wait_recv()
-            return 0
-
-        lax.fori_loop(1, n, taken, 0)
-        recv_buf[q, me] = send_buf[q, me]
+        for s in range(1, nodes):
+            to_node(q, s).wait_recv()
+        node_in[q, node] = node_out[q, node]
         total[pl.ds(pl.multiple_of(q * back, back), back), :] = jnp.sum(
-            recv_buf[q].astype(jnp.float32), axis=0
+            node_in[q].astype(jnp.float32), axis=0
         )
         return 0
 
@@ -203,17 +229,20 @@
             at = q * c_step + c * LANES
             out_ref[:, at:at + LANES] = total[pl.ds(q * back + c, t_dev, stride=per_chunk), :].astype(out_ref.dtype)
 
-    def left(s, _):
-        spread(s).wait_send()
-
-        def each(q, _):
-            give(q, s).wait_send()
-            return 0
-
-        lax.fori_loop(0, c_steps, each, 0)
-        return 0
-
-    lax.fori_loop(1, n, left, 0)
+    for s in range(1, nodes):
+        across(s).wait_send()
+    for s in range(nodes):
+        for t in range(1, lanes):
+            forward(s, t).wait_send()
+
+    def left(q, _):
+        for s in range(1, lanes):
+            to_lane(q, s).wait_send()
+        for s in range(1, nodes):
+            to_node(q, s).wait_send()
+        return 0
+
+    lax.fori_loop(0, c_steps, left, 0)
 
 
 def on_device(moe_rows, expert_ids, route_scores, gate_proj, up_proj, down_proj):
@@ -239,7 +268,6 @@
             pltpu.VMEM((ring, k_step, units), bf16),
             pltpu.VMEM((down_ring, experts_here, units, c_step), bf16),
             pltpu.VMEM((t_dev * stride, LANES), f32),
-            pltpu.VMEM((t_dev * stride, LANES), bf16),
             pltpu.VMEM((n, t_dev * stride, LANES), bf16),
             pltpu.VMEM((tokens * stride, LANES), f32),
             pltpu.VMEM((width // k_step, tokens, k_step), bf16),
@@ -248,16 +276,22 @@
             pltpu.VMEM((tokens, units), f32),
             pltpu.VMEM((experts_here, tokens, units), bf16),
             pltpu.VMEM((tokens * per_chunk, LANES), f32),
-            pltpu.VMEM((width // c_step, n, t_dev * per_chunk, LANES), bf16),
-            pltpu.VMEM((width // c_step, n, t_dev * per_chunk, LANES), bf16),
+            pltpu.VMEM((width // c_step, lanes, nodes * t_dev * per_chunk, LANES), bf16),
+            pltpu.VMEM((width // c_step, lanes, nodes * t_dev * per_chunk, LANES), bf16),
+            pltpu.VMEM((width // c_step, nodes, t_dev * per_chunk, LANES), bf16),
+            pltpu.VMEM((width // c_step, nodes, t_dev * per_chunk, LANES), bf16),
             pltpu.VMEM((t_dev * width // LANES, LANES), f32),
             pltpu.SemaphoreType.DMA((ring,)),
             pltpu.SemaphoreType.DMA((ring,)),
             pltpu.SemaphoreType.DMA((down_ring,)),
-            pltpu.SemaphoreType.DMA((n,)),
-            pltpu.SemaphoreType.DMA((n,)),
-            pltpu.SemaphoreType.DMA((width // c_step, n)),
-            pltpu.SemaphoreType.DMA((width // c_step, n)),
+            pltpu.SemaphoreType.DMA((nodes,)),
+            pltpu.SemaphoreType.DMA((nodes,)),
+            pltpu.SemaphoreType.DMA((nodes, lanes)),
+            pltpu.SemaphoreType.DMA((nodes, lanes)),
+            pltpu.SemaphoreType.DMA((width // c_step, lanes)),
+            pltpu.SemaphoreType.DMA((width // c_step, lanes)),
+            pltpu.SemaphoreType.DMA((width // c_step, nodes)),
+            pltpu.SemaphoreType.DMA((width // c_step, nodes)),
         ],
         compiler_params=pltpu.CompilerParams(
             collective_id=0, has_side_effects=True, vmem_limit_bytes=60 * 2**20

time: 51.9 us -> 46.3 us (0.89)
  Pallas kernels: 50.3 us -> 44.7 us
    pallas_call x1, Pallas kernels: 50.3 us -> 44.7 us  [on_device(): pl.pallas_call(functools.partial(kernel, (nodes, lanes, k_step, c_step, s...]
where the time goes in v2:
time: 46.3 us; the launch traced here: 46 us
  Pallas kernels  44.7 us (97%)
  local copies, waits for them, and re-layouts  1.38 us (3%)
    pallas_call x1, Pallas kernels, on_device(): pl.pallas_call(functools.partial(kernel, (nodes, lanes, k_step, c_step, s...  44.7 us
    unnamed x1, local copies, waits for them, and re-layouts  1.38 us

profile of v2, /device:TPU:0, one launch (start us, length us, event | category | flops | bytes accessed | tf_op | source)
XLA Modules:
  0.0 46.0 jit_solution(15527388445895204632)
XLA Ops:
  0.0 44.7 %shard_map.64 = bf16[2,7168]{1,0:T(2,128)(2,1)} custom-call(bf16[2,7168]{1,0:T(2,128)(2,1)} %rows_ref.1, s32[2,8]{1,0:T(2,128)} %ids_ref.1, f32[2,8]{1,0:T(2,128)} %scores_ref.1, bf16[4,7168,512]{2,1,0:T(8,128)(2,1)} %gate_hbm.1, bf16[4,7168,512]{2,1,0:T(8,128)(2,1)} %up_hbm.1, bf16[4,512,7168]{2,1,0:T(8,128)(2,1)} %down_hbm.1), custom_call_target="tpu_custom_call" | custom-call | flops 2818572288 | bytes 88080384 | tf_op jit(solution)/shard_map/pallas_call | solution.py:261
  44.7 1.4 %copy.8 = bf16[2,7168]{1,0:T(2,128)(2,1)} copy(bf16[2,7168]{1,0:T(2,128)(2,1)} %shard_map.64) | data formatting | bytes 57344
